TPU v7x, 32 devices: a whole 2x2x4 slice. The times are simulated.
32 devices in a mesh: dp: 8 (over z, y), seq: 4 (over x, core).
Axes of the slice: x: 2, y: 2, z: 4, core: 2. Of those that a mesh axis runs over, the one named last changes fastest.
Arguments:
- tokens: bfloat16 [4096, 2880], P(('dp', 'seq')), may hold values from -6 to 6
- norm_gain: bfloat16 [2880], replicated, may hold values from 0.5 to 1.5
- router_weight: bfloat16 [2880, 16], replicated, may hold values from -0.109375 to 0.109375
- expert_ids: int32 [4096, 4], P(('dp', 'seq')), may hold values from 0 to 15, all different within a row; in each aligned block of 128 rows (0 to 127, 128 to 255, ...) at most 36 rows name the same one
- gate_up_words: int32 [32, 1440, 1440], P(('dp', 'seq')), may hold values from 0 to 255
- gate_up_scales: int32 [32, 90, 1440], P(('dp', 'seq')), may hold values from 119 to 121
- down_words: int32 [32, 720, 1440], P(('dp', 'seq')), may hold values from 0 to 255
- down_scales: int32 [32, 720, 90], P(('dp', 'seq')), may hold values from 119 to 121
- cotangent: bfloat16 [4096, 2880], P(('dp', 'seq')), may hold values from -6 to 6
Outputs:
- mixed: bfloat16 [4096, 2880], P(('dp', 'seq'))
- token_grad: bfloat16 [4096, 2880], P(('dp', 'seq'))
Inputs may be any that keep to these rules, and one draw needn't show every extreme that they name: `expert_ids`: in each device's aligned block of 128 tokens no expert is named more than 36 times, a bound that some block reaches.
All inputs are finite; a program needn't handle non-finite values.
Results may differ from a plain program's by a relative error of at most 0.0029.
Values may be sent and summed in bfloat16 or wider, within the bound.
A program may use at most 192 MiB of HBM per device.

v0:
```python
import jax
import jax.numpy as jnp
from jax import lax
from jax.sharding import PartitionSpec as P

glu_slope = 1.702
norm_epsilon = 1e-05


def small_float(code_values):
    sign_part = code_values // 8
    level_code = code_values % 8
    exponent = level_code // 2
    mantissa = (level_code % 2).astype(jnp.float32)
    scaled = jnp.exp2((exponent - 1).astype(jnp.float32)) * (1.0 + 0.5 * mantissa)
    magnitude = jnp.where(exponent == 0, 0.5 * mantissa, scaled)
    return jnp.where(sign_part == 1, -magnitude, magnitude)


def unpack_rows(code_words, scale_codes):
    groups = scale_codes.shape[0]
    columns = code_words.shape[1]
    factor = jnp.exp2((scale_codes - 127).astype(jnp.float32))[:, None, :]
    shaped = code_words.reshape(groups, -1, columns)
    low_vals = (small_float(shaped % 16) * factor).astype(jnp.bfloat16)
    high_vals = (small_float(shaped // 16) * factor).astype(jnp.bfloat16)
    return jnp.stack([low_vals, high_vals], axis=2).reshape(-1, columns)


def unpack_cols(code_words, scale_codes):
    lines = code_words.shape[0]
    groups = scale_codes.shape[1]
    factor = jnp.exp2((scale_codes - 127).astype(jnp.float32))[:, :, None]
    shaped = code_words.reshape(lines, groups, -1)
    low_vals = (small_float(shaped % 16) * factor).astype(jnp.bfloat16)
    high_vals = (small_float(shaped // 16) * factor).astype(jnp.bfloat16)
    return jnp.stack([low_vals, high_vals], axis=3).reshape(lines, -1)


def expert_half(rows_in, grads_in, gate_up, down_proj):
    half_units = down_proj.shape[0]
    pre_act = jnp.dot(rows_in, gate_up, preferred_element_type=jnp.float32)
    gate_pre = pre_act[:, :half_units]
    up_pre = pre_act[:, half_units:]
    sig_gate = jax.nn.sigmoid(glu_slope * gate_pre)
    glu_gate = gate_pre * sig_gate
    active = (glu_gate * (up_pre + 1.0)).astype(jnp.bfloat16)
    part_out = jnp.dot(active, down_proj, preferred_element_type=jnp.float32).astype(jnp.bfloat16)
    back_act = lax.dot_general(
        grads_in, down_proj, (((1,), (1,)), ((), ())), preferred_element_type=jnp.float32
    )
    slope_term = sig_gate + glu_slope * glu_gate * (1.0 - sig_gate)
    grad_pre = jnp.concatenate(
        [back_act * (up_pre + 1.0) * slope_term, back_act * glu_gate], axis=1
    ).astype(jnp.bfloat16)
    part_back = lax.dot_general(
        grad_pre, gate_up, (((1,), (1,)), ((), ())), preferred_element_type=jnp.float32
    ).astype(jnp.bfloat16)
    return (part_out, part_back)


def shards(
    tokens,
    norm_gain,
    router_weight,
    expert_ids,
    gate_up_words,
    gate_up_scales,
    down_words,
    down_scales,
    cotangent,
):
    tok_count, width = tokens.shape
    top_count = expert_ids.shape[1]
    dp_count = lax.axis_size("dp")
    seq_count = lax.axis_size("seq")
    devices = dp_count * seq_count
    experts = devices // 2
    capacity = tok_count * top_count * 9 // (8 * experts)
    tok_f = tokens.astype(jnp.float32)
    cot_f = cotangent.astype(jnp.float32)
    gain_f = norm_gain.astype(jnp.float32)
    inv_rms = lax.rsqrt(jnp.mean(tok_f * tok_f, axis=1, keepdims=True) + norm_epsilon)
    normed = (tok_f * inv_rms * gain_f).astype(jnp.bfloat16)
    logits = jnp.dot(normed, router_weight, preferred_element_type=jnp.float32)
    expert_cols = lax.broadcasted_iota(jnp.int32, (tok_count, top_count, experts), 2)
    one_hot = expert_ids[:, :, None] == expert_cols
    picked = jnp.sum(jnp.where(one_hot, logits[:, None, :], 0.0), axis=2)
    raised = jnp.exp(picked)
    probs = raised / jnp.sum(raised, axis=1, keepdims=True)
    flat_probs = probs.reshape(-1)
    pair_count = tok_count * top_count
    flat_hot = one_hot.reshape(pair_count, experts).astype(jnp.int32)
    running = jnp.cumsum(flat_hot, axis=0)
    slot_of = jnp.sum(running * flat_hot, axis=1) - 1
    target = expert_ids.reshape(-1) * capacity + slot_of
    pair_index = jnp.arange(pair_count, dtype=jnp.int32)
    table = jnp.full((experts * capacity,), pair_count, jnp.int32).at[target].set(pair_index)
    filled = table < pair_count
    safe_pair = jnp.minimum(table, pair_count - 1)
    safe_token = safe_pair // top_count
    slot_rows = jnp.where(filled[:, None], normed[safe_token], 0)
    slot_grads = jnp.where(
        filled[:, None],
        (flat_probs[safe_pair][:, None] * cot_f[safe_token]).astype(jnp.bfloat16),
        0,
    )
    gate_up = unpack_rows(gate_up_words[0], gate_up_scales[0])
    down_proj = unpack_cols(down_words[0], down_scales[0])

    def spread(slot_values):
        return jnp.broadcast_to(
            slot_values.reshape(experts, 1, capacity, width), (experts, 2, capacity, width)
        ).reshape(devices, capacity, width)

    rows_in = lax.all_to_all(
        spread(slot_rows), ("dp", "seq"), split_axis=0, concat_axis=0, tiled=True
    )
    grads_in = lax.all_to_all(
        spread(slot_grads), ("dp", "seq"), split_axis=0, concat_axis=0, tiled=True
    )
    layout = rows_in.shape
    part_out, part_back = expert_half(
        rows_in.reshape(-1, width), grads_in.reshape(-1, width), gate_up, down_proj
    )
    part_out, part_back = (part_out.reshape(layout), part_back.reshape(layout))
    back_out, back_grad = (
        lax.all_to_all(part_out, ("dp", "seq"), split_axis=0, concat_axis=0, tiled=True),
        lax.all_to_all(part_back, ("dp", "seq"), split_axis=0, concat_axis=0, tiled=True),
    )
    out_slots = jnp.sum(
        back_out.reshape(experts, 2, capacity, width).astype(jnp.float32), axis=1
    ).reshape(experts * capacity, width)
    grad_slots = jnp.sum(
        back_grad.reshape(experts, 2, capacity, width).astype(jnp.float32), axis=1
    ).reshape(experts * capacity, width)
    pair_out = out_slots[target].reshape(tok_count, top_count, width)
    pair_back = grad_slots[target].reshape(tok_count, top_count, width)
    mixed = (tok_f + jnp.sum(probs[:, :, None] * pair_out, axis=1)).astype(jnp.bfloat16)
    dprob = jnp.sum(cot_f[:, None, :] * pair_out, axis=2)
    dpicked = probs * (dprob - jnp.sum(probs * dprob, axis=1, keepdims=True))
    dlogits = jnp.sum(jnp.where(one_hot, dpicked[:, :, None], 0.0), axis=1)
    dnormed = jnp.dot(
        dlogits, router_weight.astype(jnp.float32).T, precision=lax.Precision.HIGHEST
    ) + jnp.sum(pair_back, axis=1)
    gain_grad = gain_f * dnormed
    token_grad = (
        cot_f
        + inv_rms * gain_grad
        - tok_f * (inv_rms * inv_rms * inv_rms) * jnp.mean(gain_grad * tok_f, axis=1, keepdims=True)
    )
    return (mixed, token_grad.astype(jnp.bfloat16))


def solution(mesh):
    in_specs = (
        P(("dp", "seq"), None),
        P(),
        P(),
        P(("dp", "seq"), None),
        P(("dp", "seq"), None, None),
        P(("dp", "seq"), None, None),
        P(("dp", "seq"), None, None),
        P(("dp", "seq"), None, None),
        P(("dp", "seq"), None),
    )
    out_specs = (P(("dp", "seq"), None), P(("dp", "seq"), None))
    return jax.shard_map(shards, mesh=mesh, in_specs=in_specs, out_specs=out_specs, check_vma=False)
```

profile of v0, /device:TPU:0, one launch (start us, length us, event | category | flops | bytes accessed | tf_op | source)
XLA Modules:
  0.0 1011.0 jit_solution(9308398401097125571)
XLA Ops:
  13.4 6.6 gather.24
  46.0 7.6 all-to-all-start
  54.6 183.4 %multiply_convert_fusion.1 = (bf16[90,16,1,1440]{3,2,1,0:T(2,128)(2,1)}, s32[90,16,1,1440]{3,2,1,0:T(1,128)}) fusion(f32[90,1440]{1,0:T(8,128)S(1)} %bitcast.52, s32[90,16,1,1440]{3,1,0,2:T(8,128)} %bitcast.45), kind=kLoop, calls=%fused_computation.45 | loop fusion | flops 130636800 | bytes 21254400 | tf_op jit(solution)/shard_map/convert_element_type | solution.py:25
  243.6 6.3 all-to-all-start.2
  249.9 189.6 %multiply_convert_fusion = bf16[90,16,1,1440]{3,2,1,0:T(2,128)(2,1)S(1)} fusion(s32[90,16,1,1440]{3,2,1,0:T(1,128)} %get-tuple-element.5, f32[90,1440]{1,0:T(8,128)S(1)} %bitcast.53, s32[90,16,1,1440]{3,1,0,2:T(8,128)} %bitcast.46), kind=kLoop, calls=%fused_computation.44 | loop fusion | flops 132710400 | bytes 21254400 | tf_op jit(solution)/shard_map/convert_element_type | solution.py:26
  439.5 22.8 %pad_maximum_fusion = bf16[90,16,2,1440]{3,2,1,0:T(2,128)(2,1)} fusion(bf16[90,16,1,1440]{3,2,1,0:T(2,128)(2,1)S(1)} %multiply_convert_fusion, bf16[90,16,1,1440]{3,2,1,0:T(2,128)(2,1)} %get-tuple-element.4), kind=kLoop, calls=%fused_computation.43 | loop fusion | flops 16588800 | bytes 16588800 | tf_op jit(solution)/shard_map/stack | solution.py:27
  462.3 18.6 %reshape.1154 = bf16[2880,1440]{1,0:T(8,128)(2,1)} reshape(bf16[90,16,2,1440]{3,2,1,0:T(2,128)(2,1)} %pad_maximum_fusion) | data formatting | bytes 16588800 | tf_op jit(solution)/shard_map/reshape | solution.py:27
  487.3 24.6 %fusion.8 = (bf16[720,90,16,1]{0,2,1,3:T(8,128)(2,1)S(1)}, bf16[720,90,16,1]{0,2,1,3:T(8,128)(2,1)S(1)}) fusion(s32[720,90,16,1]{0,2,1,3:T(8,128)} %bitcast.49, f32[720,90]{0,1:T(8,128)S(1)} %bitcast.54), kind=kLoop, calls=%fused_computation.80 | loop fusion | flops 127526400 | bytes 8553600 | tf_op jit(solution)/shard_map/convert_element_type | solution.py:35
  514.4 9.5 copy.83
  523.9 10.1 reshape.1155
  534.0 9.4 reshape.1153
  543.4 17.9 %fusion.45 = f32[1152,1440]{0,1:T(8,128)} fusion(bf16[1152,2880]{1,0:T(8,128)(2,1)} %reshape.1153, bf16[2880,1440]{1,0:T(8,128)(2,1)} %reshape.1154), kind=kOutput, calls=%fused_computation.169 | convolution fusion | flops 9555148800 | bytes 21565440 | tf_op jit(solution)/shard_map/dot_general | solution.py:42
  561.3 9.5 reshape.1160
  570.8 12.5 %multiply_convert_fusion.4 = (bf16[1152,720]{0,1:T(8,128)(2,1)S(1)}, bf16[1152,720]{0,1:T(8,128)(2,1)S(1)}) fusion(f32[1152,1440]{0,1:T(8,128)} %fusion.45, bf16[1152,2880]{1,0:T(8,128)(2,1)} %reshape.1160, bf16[720,2880]{0,1:T(8,128)(2,1)} %reshape.1155), kind=kOutput, calls=%fused_computation.108 | convolution fusion | flops 4790016000 | bytes 20736000 | tf_op jit(solution)/shard_map/dot_general | solution.py:49
  583.4 13.3 %convolution_convert_fusion.1 = bf16[1152,2880]{0,1:T(8,128)(2,1)} fusion(bf16[2880,1440]{1,0:T(8,128)(2,1)S(1)} %bitcast.51, bf16[1152,720]{0,1:T(8,128)(2,1)S(1)} %get-tuple-element.7, bf16[1152,720]{0,1:T(8,128)(2,1)S(1)} %get-tuple-element.6), kind=kOutput, calls=%fused_computation.38 | convolution fusion | flops 9565102080 | bytes 18247680 | tf_op jit(solution)/shard_map/dot_general | solution.py:56
  596.7 10.1 copy.91
  606.8 8.7 reshape.1161
  621.5 11.7 %convolution_convert_fusion = bf16[1152,2880]{0,1:T(8,128)(2,1)} fusion(bf16[720,2880]{0,1:T(8,128)(2,1)} %reshape.1155, f32[1152,1440]{0,1:T(8,128)} %fusion.45), kind=kOutput, calls=%fused_computation.37 | convolution fusion | flops 4787527680 | bytes 17418240 | tf_op jit(solution)/shard_map/dot_general | solution.py:48
  633.2 10.1 copy.84
  643.3 8.7 reshape.1156
  652.0 136.9 %all-to-all-done.3 = bf16[32,36,2880]{2,1,0:T(8,128)(2,1)} async-done(((bf16[32,36,2880]{2,1,0:T(8,128)(2,1)}), bf16[32,36,2880]{2,1,0:T(8,128)(2,1)}, u32[]{:S(2)}, u32[]{:S(2)}) %all-to-all-start.3) | async-done | bytes 6635552 | tf_op jit(solution)/shard_map/all_to_all | solution.py:129
  792.8 8.2 convert_reduce_fusion
  801.0 6.4 reshape.1162
  807.5 9.9 gather_fusion.4
  817.4 7.7 reshape.1163
  825.1 6.3 reduce_sum.118
  832.9 127.3 %all-to-all-done.1 = bf16[32,36,2880]{2,1,0:T(8,128)(2,1)} async-done(((bf16[32,36,2880]{2,1,0:T(8,128)(2,1)}), bf16[32,36,2880]{2,1,0:T(8,128)(2,1)}, u32[]{:S(2)}, u32[]{:S(2)}) %all-to-all-start.1) | async-done | bytes 6635552 | tf_op jit(solution)/shard_map/all_to_all | solution.py:128
  960.2 8.3 convert_reduce_fusion.1
  968.5 6.4 reshape.1157
  974.9 10.1 %gather_fusion.1 = f32[512,2880]{1,0:T(8,128)} fusion(f32[576,2880]{1,0:T(8,128)} %reshape.1157, s32[1024]{0:T(1024)S(1)} %pad_clamp_fusion.1), kind=kCustom, calls=%fused_computation.1 | custom fusion | bytes 11798528 | tf_op jit(solution)/shard_map/gather | solution.py:137
  985.0 7.8 reshape.1158
  992.9 8.7 multiply_reduce_fusion
  (117 shorter events, 74.5 us)
Async XLA Ops:
  0.6 21.3 %copy-start = (bf16[2880,16]{0,1:T(8,128)(2,1)S(1)}, bf16[2880,16]{0,1:T(8,128)(2,1)}, u32[]{:S(2)}) copy-start(bf16[2880,16]{0,1:T(8,128)(2,1)} %param.11) | copy-start | bytes 276484
  4.1 2.5 copy-start.19
  8.1 5.4 copy-start.1
  13.4 6.6 copy-start.21
  13.4 6.6 copy-start.3
  20.0 2.2 copy-start.15
  20.0 7.0 copy-start.11
  21.0 0.5 copy-start.22
  22.2 0.6 copy-start.13
  22.2 9.4 copy-start.17
  22.9 8.8 copy-start.7
  46.0 7.6 copy-start.9
  46.0 192.0 %all-to-all-start = ((bf16[32,36,2880]{2,1,0:T(8,128)(2,1)}), bf16[32,36,2880]{2,1,0:T(8,128)(2,1)}, u32[]{:S(2)}, u32[]{:S(2)}) async-start(bf16[32,36,2880]{2,1,0:T(8,128)(2,1)} %bitcast.48), calls=%async_computation | async-start | bytes 15073280 | tf_op jit(solution)/shard_map/all_to_all | solution.py:116
  243.6 317.7 %all-to-all-start.2 = ((bf16[32,36,2880]{2,1,0:T(8,128)(2,1)}), bf16[32,36,2880]{2,1,0:T(8,128)(2,1)}, u32[]{:S(2)}, u32[]{:S(2)}) async-start(bf16[32,36,2880]{2,1,0:T(8,128)(2,1)} %bitcast.47), calls=%async_computation.2 | async-start | bytes 15073280 | tf_op jit(solution)/shard_map/all_to_all | solution.py:119
  480.9 5.9 copy-start.10
  561.3 22.0 %slice-start = ((s8[8847360]{0:T(1024)(128)(4,1)}), s8[458752]{0:T(1024)(128)(4,1)S(1)}, s32[]{:S(2)}) async-start(s8[8847360]{0:T(1024)(128)(4,1)} %bitcast.50), calls=%async_computation.4 | async-start | bytes 917504
  570.8 12.6 %slice-start.1 = ((s8[8847360]{0:T(1024)(128)(4,1)}), s8[4194304]{0:T(1024)(128)(4,1)S(1)}, s32[]{:S(2)}) async-start(s8[8847360]{0:T(1024)(128)(4,1)} %bitcast.50), calls=%async_computation.5 | async-start | bytes 8388608
  570.8 12.6 %slice-start.2 = ((s8[8847360]{0:T(1024)(128)(4,1)}), s8[4194304]{0:T(1024)(128)(4,1)S(1)}, s32[]{:S(2)}) async-start(s8[8847360]{0:T(1024)(128)(4,1)} %bitcast.50), calls=%async_computation.6 | async-start | bytes 8388608
  615.5 173.5 %all-to-all-start.3 = ((bf16[32,36,2880]{2,1,0:T(8,128)(2,1)}), bf16[32,36,2880]{2,1,0:T(8,128)(2,1)}, u32[]{:S(2)}, u32[]{:S(2)}) async-start(bf16[32,36,2880]{2,1,0:T(8,128)(2,1)} %reshape.1161), calls=%async_computation.3 | async-start | bytes 15073280 | tf_op jit(solution)/shard_map/all_to_all | solution.py:129
  652.0 140.8 %copy-start.20 = (s32[512,1]{0,1:T(1,128)S(1)}, s32[512,1]{0,1:T(1,128)}, u32[]{:S(2)}) copy-start(s32[512,1]{0,1:T(1,128)} %copy-done.19) | copy-start | bytes 6148
  788.9 171.3 %all-to-all-start.1 = ((bf16[32,36,2880]{2,1,0:T(8,128)(2,1)}), bf16[32,36,2880]{2,1,0:T(8,128)(2,1)}, u32[]{:S(2)}, u32[]{:S(2)}) async-start(bf16[32,36,2880]{2,1,0:T(8,128)(2,1)} %reshape.1156), calls=%async_computation.1 | async-start | bytes 15073280 | tf_op jit(solution)/shard_map/all_to_all | solution.py:128
  985.0 7.8 copy-start.2
  985.0 7.8 copy-start.8
  992.8 8.9 copy-start.14
  992.8 8.9 copy-start.18
  992.8 8.9 copy-start.16
  992.9 8.9 copy-start.4
  992.9 8.9 copy-start.12
  1001.6 3.9 copy-start.5
  1001.6 5.5 copy-start.6
  1001.6 5.5 copy-start.23
  1001.6 5.5 copy-start.24
where the time goes:
time: 1020 us; the launch traced here: 1010 us
  other arithmetic  469 us (46%)
  waiting for transfers between devices  264 us (26%)
  local copies, waits for them, and re-layouts  193 us (19%)
  matrix products  59.4 us (6%)
  starting transfers between devices  23.9 us (2%)
    convert_element_type x1, other arithmetic, unpack_rows(): high_vals = (small_float(shaped // 16) * factor).astype(jnp.bfloat16)  190 us
    convert_element_type x1, other arithmetic, unpack_rows(): low_vals = (small_float(shaped % 16) * factor).astype(jnp.bfloat16)  183 us
    all_to_all x1, waiting for transfers between devices, shards(): lax.all_to_all(part_back, ('dp', 'seq'), split_axis=0, concat_axis=0, til...  137 us
    all_to_all x1, waiting for transfers between devices, shards(): lax.all_to_all(part_out, ('dp', 'seq'), split_axis=0, concat_axis=0, tile...  127 us
    convert_element_type x1, other arithmetic, unpack_cols(): low_vals = (small_float(shaped % 16) * factor).astype(jnp.bfloat16)  24.6 us
    another operation x1, other arithmetic, unpack_rows(): return jnp.stack([low_vals, high_vals], axis=2).reshape(-1, columns)  22.8 us
  transfers between devices with their start and end apart: 4, of which 2 were waited for; matrix products, arithmetic and copies ran while one was open for 56% of the time, Pallas kernels for 0%

commit v1 on v0

v1 whole, which is shorter than its diff:
```python
import jax
import jax.numpy as jnp
from jax import lax
from jax.experimental import pallas as pl
from jax.experimental.pallas import tpu as pltpu
from jax.sharding import PartitionSpec as P

glu_slope = 1.702
norm_epsilon = 1e-05


def small_float(codes):
    level = (codes & 7).astype(jnp.float32)
    magnitude = jnp.maximum(jnp.maximum(0.5 * level, level - 2.0), 2.0 * level - 8.0)
    return jnp.where(codes >= 8, -magnitude, magnitude)


def decode_kernel(words_ref, factor_ref, out_ref, wide_ref):
    columns = words_ref.shape[1]
    for group in range(factor_ref.shape[1]):
        for number, start in enumerate(range(0, columns, 128)):
            lanes = min(128, columns - start)
            words = words_ref[pl.ds(16 * group, 16), pl.ds(start, lanes)]
            factor = factor_ref[0, pl.ds(group, 1), pl.ds(start, lanes)]
            low_vals = small_float(words & 15) * factor
            high_vals = small_float(words >> 4) * factor
            if lanes < 128:
                rest = jnp.zeros((16, 128 - lanes), jnp.float32)
                low_vals = jnp.concatenate([low_vals, rest], axis=1)
                high_vals = jnp.concatenate([high_vals, rest], axis=1)
            slot = wide_ref.at[number]
            slot[pl.ds(0, 16, stride=2), :] = low_vals
            slot[pl.ds(1, 16, stride=2), :] = high_vals
            out_ref[pl.ds(32 * group, 32), pl.ds(start, lanes)] = slot[:, :lanes].astype(jnp.bfloat16)


def unpack_rows(code_words, scale_codes):
    groups, columns = scale_codes.shape
    at_once = 10 if groups % 10 == 0 else 1
    factor = jnp.exp2((scale_codes - 127).astype(jnp.float32))
    return pl.pallas_call(
        decode_kernel,
        grid=(groups // at_once,),
        in_specs=[
            pl.BlockSpec((16 * at_once, columns), lambda step: (step, 0)),
            pl.BlockSpec((1, at_once, columns), lambda step: (step, 0, 0)),
        ],
        out_specs=pl.BlockSpec((32 * at_once, columns), lambda step: (step, 0)),
        out_shape=jax.ShapeDtypeStruct((32 * groups, columns), jnp.bfloat16),
        scratch_shapes=[pltpu.VMEM((-(-columns // 128), 32, 128), jnp.float32)],
        compiler_params=pltpu.CompilerParams(vmem_limit_bytes=24 * 1024 * 1024),
        cost_estimate=pl.CostEstimate(
            flops=16 * 32 * groups * columns, bytes_accessed=8 * 16 * groups * columns, transcendentals=0
        ),
    )(code_words, factor.reshape(groups // at_once, at_once, columns))


def expert_half(rows_in, grads_in, gate_up, down_turned):
    half_units = down_turned.shape[1]
    pre_act = jnp.dot(rows_in, gate_up, preferred_element_type=jnp.float32)
    gate_pre = pre_act[:, :half_units]
    up_pre = pre_act[:, half_units:]
    sig_gate = jax.nn.sigmoid(glu_slope * gate_pre)
    glu_gate = gate_pre * sig_gate
    active = (glu_gate * (up_pre + 1.0)).astype(jnp.bfloat16)
    part_out = lax.reduce_precision(
        lax.dot_general(
            active, down_turned, (((1,), (1,)), ((), ())), preferred_element_type=jnp.float32
        ),
        8,
        7,
    ).astype(jnp.bfloat16)
    back_act = jnp.dot(grads_in, down_turned, preferred_element_type=jnp.float32)
    slope_term = sig_gate + glu_slope * glu_gate * (1.0 - sig_gate)
    grad_pre = jnp.concatenate(
        [back_act * (up_pre + 1.0) * slope_term, back_act * glu_gate], axis=1
    ).astype(jnp.bfloat16)
    part_back = lax.reduce_precision(
        lax.dot_general(
            grad_pre, gate_up, (((1,), (1,)), ((), ())), preferred_element_type=jnp.float32
        ),
        8,
        7,
    ).astype(jnp.bfloat16)
    return (part_out, part_back)


def shards(
    tokens,
    norm_gain,
    router_weight,
    expert_ids,
    gate_up_words,
    gate_up_scales,
    down_words,
    down_scales,
    cotangent,
):
    tok_count, width = tokens.shape
    top_count = expert_ids.shape[1]
    dp_count = lax.axis_size("dp")
    seq_count = lax.axis_size("seq")
    devices = dp_count * seq_count
    experts = devices // 2
    capacity = -(-(tok_count * top_count * 9 // (8 * experts)) // 8) * 8
    tok_f = tokens.astype(jnp.float32)
    cot_f = cotangent.astype(jnp.float32)
    gain_f = norm_gain.astype(jnp.float32)
    inv_rms = lax.rsqrt(jnp.mean(tok_f * tok_f, axis=1, keepdims=True) + norm_epsilon)
    normed = (tok_f * inv_rms * gain_f).astype(jnp.bfloat16)
    logits = jnp.dot(normed, router_weight, preferred_element_type=jnp.float32)
    expert_cols = lax.broadcasted_iota(jnp.int32, (tok_count, top_count, experts), 2)
    one_hot = expert_ids[:, :, None] == expert_cols
    picked = jnp.sum(jnp.where(one_hot, logits[:, None, :], 0.0), axis=2)
    raised = jnp.exp(picked)
    probs = raised / jnp.sum(raised, axis=1, keepdims=True)

    slots = experts * capacity
    named = jnp.any(one_hot, axis=1)
    earlier = (
        lax.broadcasted_iota(jnp.int32, (tok_count, tok_count), 1)
        < lax.broadcasted_iota(jnp.int32, (tok_count, tok_count), 0)
    )
    before = jnp.dot(
        earlier.astype(jnp.bfloat16), named.astype(jnp.bfloat16), preferred_element_type=jnp.float32
    )
    slot_of = jnp.sum(jnp.where(one_hot, before[:, None, :], 0.0), axis=2).astype(jnp.int32)
    target = expert_ids * capacity + slot_of
    slot_cols = lax.broadcasted_iota(jnp.int32, (tok_count, slots), 1)
    place = jnp.zeros((tok_count, slots), jnp.bool_)
    weight = jnp.zeros((tok_count, slots), jnp.float32)
    for k in range(top_count):
        hit = target[:, k : k + 1] == slot_cols
        place = place | hit
        weight = jnp.where(hit, probs[:, k : k + 1], weight)
    place_b = place.astype(jnp.bfloat16)
    to_slots = (((0,), (0,)), ((), ()))
    slot_rows = lax.dot_general(
        place_b, normed, to_slots, preferred_element_type=jnp.float32
    ).astype(jnp.bfloat16)
    slot_cot = lax.dot_general(place_b, cotangent, to_slots, preferred_element_type=jnp.float32)
    slot_prob = jnp.sum(weight, axis=0)[:, None]
    slot_grads = lax.reduce_precision(slot_prob * slot_cot, 8, 7).astype(jnp.bfloat16)
    gate_up = unpack_rows(gate_up_words[0], gate_up_scales[0])
    down_turned = unpack_rows(down_words[0].T, down_scales[0].T)

    both = jnp.stack(
        [
            slot_rows.reshape(experts, capacity, width),
            slot_grads.reshape(experts, capacity, width),
        ],
        axis=1,
    ).reshape(devices, capacity, width)
    mine = lax.all_to_all(both, ("dp", "seq"), split_axis=0, concat_axis=0, tiled=True)
    mine = mine.reshape(devices * capacity, width)
    swap = [(i, i ^ 1) for i in range(seq_count)]
    other = lax.ppermute(mine, "seq", swap)
    first = lax.rem(lax.axis_index("seq"), 2) == 0
    rows_in = jnp.where(first, mine, other)
    grads_in = jnp.where(first, other, mine)
    part_out, part_back = expert_half(rows_in, grads_in, gate_up, down_turned)
    back_out = lax.all_to_all(
        part_out.reshape(devices, capacity, width), ("dp", "seq"), split_axis=0, concat_axis=0, tiled=True
    ).reshape(2 * slots, width)
    back_grad = lax.all_to_all(
        part_back.reshape(devices, capacity, width), ("dp", "seq"), split_axis=0, concat_axis=0, tiled=True
    ).reshape(2 * slots, width)

    half_target = expert_ids * (2 * capacity) + slot_of
    half_cols = lax.broadcasted_iota(jnp.int32, (tok_count, 2 * slots), 1)
    hits = []
    place_half = jnp.zeros((tok_count, 2 * slots), jnp.bool_)
    weight_half = jnp.zeros((tok_count, 2 * slots), jnp.float32)
    for k in range(top_count):
        start = half_target[:, k : k + 1]
        hit = (start == half_cols) | (start + capacity == half_cols)
        hits.append(hit)
        place_half = place_half | hit
        weight_half = jnp.where(hit, probs[:, k : k + 1], weight_half)
    weight_high = lax.reduce_precision(weight_half, 8, 7)
    weight_low = weight_half - weight_high
    mix = jnp.dot(
        weight_high.astype(jnp.bfloat16), back_out, preferred_element_type=jnp.float32
    ) + jnp.dot(weight_low.astype(jnp.bfloat16), back_out, preferred_element_type=jnp.float32)
    mixed = (tok_f + mix).astype(jnp.bfloat16)
    dots = lax.dot_general(
        cotangent, back_out, (((1,), (1,)), ((), ())), preferred_element_type=jnp.float32
    )
    dprob = jnp.stack([jnp.sum(jnp.where(hit, dots, 0.0), axis=1) for hit in hits], axis=1)
    dpicked = probs * (dprob - jnp.sum(probs * dprob, axis=1, keepdims=True))
    dlogits = jnp.sum(jnp.where(one_hot, dpicked[:, :, None], 0.0), axis=1)
    dnormed = jnp.dot(
        dlogits, router_weight.astype(jnp.float32).T, precision=lax.Precision.HIGHEST
    ) + jnp.dot(
        place_half.astype(jnp.bfloat16), back_grad, preferred_element_type=jnp.float32
    )
    gain_grad = gain_f * dnormed
    token_grad = (
        cot_f
        + inv_rms * gain_grad
        - tok_f * (inv_rms * inv_rms * inv_rms) * jnp.mean(gain_grad * tok_f, axis=1, keepdims=True)
    )
    return (mixed, token_grad.astype(jnp.bfloat16))


def solution(mesh):
    in_specs = (
        P(("dp", "seq"), None),
        P(),
        P(),
        P(("dp", "seq"), None),
        P(("dp", "seq"), None, None),
        P(("dp", "seq"), None, None),
        P(("dp", "seq"), None, None),
        P(("dp", "seq"), None, None),
        P(("dp", "seq"), None),
    )
    out_specs = (P(("dp", "seq"), None), P(("dp", "seq"), None))
    return jax.shard_map(shards, mesh=mesh, in_specs=in_specs, out_specs=out_specs, check_vma=False)
```

time: 1020 us -> 659 us (0.65)
  other arithmetic: 469 us -> 12.5 us
  blocking collectives: 0 us -> 174 us
  local copies, waits for them, and re-layouts: 193 us -> 63.5 us
  matrix products: 59.4 us -> 94.7 us
  waiting for transfers between devices: 264 us -> 283 us
  starting transfers between devices: 23.9 us -> 7.55 us
  Pallas kernels: 0 us -> 15.4 us
    convert_element_type x5 -> x0, other arithmetic: 398 us -> none  [the longest x1 190 us: unpack_rows(): high_vals = (small_float(shaped // 16) * factor).astype(jnp.bfloat16)]
    all_to_all x0 -> x1, blocking collectives: none -> 174 us  [shards(): lax.all_to_all(both, ('dp', 'seq'), split_axis=0, concat_axis=0, tiled=True)]
    reshape x10 -> x2, local copies, waits for them, and re-layouts: 93.2 us -> 10.2 us  [the longest x1 10.2 us: shards(): mine = mine.reshape(devices * capacity, width)]
    gather x7 -> x0, local copies, waits for them, and re-layouts: 45 us -> none  [the longest x2 11.9 us: shards(): cot_f[safe_token]]
    reduce_sum x6 -> x2, other arithmetic: 31.6 us -> 0.99 us  [the longest x1 0.78 us: shards(): jnp.sum(jnp.where(one_hot, before[:, None, :], 0.0), axis=2)]
    dot_general x2 -> x9, matrix products: 24.2 us -> 54.1 us  [the longest x1 12.9 us: expert_half(): jnp.dot(grads_in, down_turned, preferred_element_type=jnp.float32)]
    another operation x4 -> x1, other arithmetic: 26.6 us -> 3.99 us  [shards(): jnp.stack([slot_rows.reshape(experts, capacity, width), slot_grads.reshap...]
    all_to_all x4 -> x2, waiting for transfers between devices: 264 us -> 283 us  [the longest x1 155 us: shards(): lax.all_to_all(part_back.reshape(devices, capacity, width), ('dp', 'seq')...]
  transfers between devices with their start and end apart: 4 -> 3, of which waited for: 2 -> 2; matrix products, arithmetic and copies ran while one was open for 56% -> 9% of each run, Pallas kernels for 0% -> 2%
where the time goes in v1:
time: 659 us; the launch traced here: 652 us
  waiting for transfers between devices  283 us (43%)
  blocking collectives  174 us (26%)
  matrix products  94.7 us (14%)
  local copies, waits for them, and re-layouts  63.5 us (10%)
  Pallas kernels  15.4 us (2%)
  other arithmetic  12.5 us (2%)
  starting transfers between devices  7.55 us (1%)
    all_to_all x1, blocking collectives, shards(): lax.all_to_all(both, ('dp', 'seq'), split_axis=0, concat_axis=0, tiled=True)  174 us
    all_to_all x1, waiting for transfers between devices, shards(): lax.all_to_all(part_back.reshape(devices, capacity, width), ('dp', 'seq')...  155 us
    all_to_all x1, waiting for transfers between devices, shards(): lax.all_to_all(part_out.reshape(devices, capacity, width), ('dp', 'seq'),...  128 us
    dot_general x1, matrix products, expert_half(): pre_act = jnp.dot(rows_in, gate_up, preferred_element_type=jnp.float32)  21.8 us
    unnamed x24, local copies, waits for them, and re-layouts  16.2 us
    dot_general x1, matrix products, expert_half(): lax.dot_general(grad_pre, gate_up, (((1,), (1,)), ((), ())), preferred_el...  16 us
    pallas_call x2, Pallas kernels, unpack_rows(): pl.pallas_call(decode_kernel, grid=(groups // at_once,), in_specs=[pl.Blo...  15.4 us
  transfers between devices with their start and end apart: 3, of which 2 were waited for; matrix products, arithmetic and copies ran while one was open for 9% of the time, Pallas kernels for 2%

profile of v1, /device:TPU:0, one launch (start us, length us, event | category | flops | bytes accessed | tf_op | source)
XLA Modules:
  0.0 652.5 jit_solution(18330937917260435826)
XLA Ops:
  0.6 1.5 fusion.13
  3.8 1.7 fusion.57
  7.0 4.3 convolution_convert_fusion
  11.5 3.1 reduce-precision_convert_fusion.2
  14.6 6.2 copy.40
  20.8 6.2 copy.39
  26.9 4.0 pad_maximum_fusion
  30.9 3.6 copy.41
  34.5 174.4 %all_to_all.15 = bf16[32,40,2880]{2,1,0:T(8,128)(2,1)} all-to-all(bf16[32,40,2880]{2,1,0:T(8,128)(2,1)} %bitcast.73), channel_id=1, replica_groups=mesh['dp'=8,'seq'=4] {'dp','seq'}, dimensions={0} | all-to-all | bytes 14745600 | tf_op jit(solution)/shard_map/all_to_all | solution.py:154
  208.9 10.2 %copy.43 = bf16[1280,2880]{0,1:T(8,128)(2,1)} copy(bf16[1280,2880]{1,0:T(8,128)(2,1)} %bitcast.74) | data formatting | bytes 14745600 | tf_op jit(solution)/shard_map/reshape | solution.py:155
  219.6 2.0 exponential_reduce_fusion
  221.7 5.9 copy.44
  227.6 2.3 copy-done.1
  229.8 5.2 shard_map.105
  235.1 5.1 copy-done.2
  240.2 10.2 %shard_map.104 = bf16[2880,1440]{1,0:T(8,128)(2,1)S(1)} custom-call(s32[1440,1440]{1,0:T(8,128)S(1)} %bitcast.70, f32[9,10,1440]{2,1,0:T(8,128)S(1)} %exp2.34.factor_ref), custom_call_target="tpu_custom_call" | custom-call | flops 66355200 | bytes 16588800 | tf_op jit(solution)/shard_map/pallas_call | solution.py:41
  250.4 21.8 %fusion.2 = f32[1280,1440]{0,1:T(8,128)S(1)} fusion(bf16[2880,1440]{1,0:T(8,128)(2,1)S(1)} %shard_map.104, bf16[1280,2880]{0,1:T(8,128)(2,1)} %copy.43, bf16[1280,2880]{0,1:T(8,128)(2,1)} %collective-permute-done, pred[]{:T(512)S(6)} %eq.157), kind=kOutput, calls=%fused_computation.5 | convolution fusion | flops 10620518400 | bytes 30412800 | tf_op jit(solution)/shard_map/dot_general | solution.py:60
  272.2 2.9 copy-done.10
  275.1 8.3 %reduce-precision_convert_fusion.1 = bf16[1280,2880]{0,1:T(8,128)(2,1)} fusion(bf16[2880,720]{1,0:T(8,128)(2,1)S(1)} %shard_map.105, f32[1280,1440]{0,1:T(8,128)S(1)} %fusion.2), kind=kOutput, calls=%fused_computation.1 | convolution fusion | flops 5323161600 | bytes 18892800 | tf_op jit(solution)/shard_map/dot_general | solution.py:67
  283.4 10.6 %copy.45 = bf16[1280,2880]{1,0:T(8,128)(2,1)} copy(bf16[1280,2880]{0,1:T(8,128)(2,1)} %reduce-precision_convert_fusion.1) | data formatting | bytes 14745600 | tf_op jit(solution)/shard_map/convert_element_type | solution.py:72
  294.0 3.7 all-to-all-start.1
  297.7 12.9 %multiply_convert_fusion.1 = (bf16[1280,720]{0,1:T(8,128)(2,1)S(1)}, bf16[1280,720]{0,1:T(8,128)(2,1)S(1)}) fusion(f32[1280,1440]{0,1:T(8,128)} %copy-done.10, bf16[2880,720]{1,0:T(8,128)(2,1)} %copy-done.4, bf16[1280,2880]{0,1:T(8,128)(2,1)} %collective-permute-done, bf16[1280,2880]{0,1:T(8,128)(2,1)} %copy.43, pred[]{:T(512)S(6)} %eq.157), kind=kOutput, calls=%fused_computation.18 | convolution fusion | flops 5325926400 | bytes 29952000 | tf_op jit(solution)/shard_map/dot_general | solution.py:73
  310.6 16.0 %reduce-precision_convert_fusion = bf16[1280,2880]{0,1:T(8,128)(2,1)} fusion(bf16[2880,1440]{1,0:T(8,128)(2,1)} %copy-done.3, bf16[1280,720]{0,1:T(8,128)(2,1)S(1)} %get-tuple-element.9, bf16[1280,720]{0,1:T(8,128)(2,1)S(1)} %get-tuple-element.8), kind=kOutput, calls=%fused_computation | convolution fusion | flops 10631577600 | bytes 19353600 | tf_op jit(solution)/shard_map/dot_general | solution.py:79
  326.6 10.4 %copy.47 = bf16[1280,2880]{1,0:T(8,128)(2,1)} copy(bf16[1280,2880]{0,1:T(8,128)(2,1)} %reduce-precision_convert_fusion) | data formatting | bytes 14745600 | tf_op jit(solution)/shard_map/convert_element_type | solution.py:84
  337.1 128.0 %all-to-all-done.1 = bf16[32,40,2880]{2,1,0:T(8,128)(2,1)} async-done(((bf16[32,40,2880]{2,1,0:T(8,128)(2,1)}), bf16[32,40,2880]{2,1,0:T(8,128)(2,1)}, u32[]{:S(2)}, u32[]{:S(2)}) %all-to-all-start.1) | async-done | bytes 7372832 | tf_op jit(solution)/shard_map/all_to_all | solution.py:162
  465.1 3.9 all-to-all-start.2
  469.0 6.3 fusion.30
  475.3 5.7 select_reduce_fusion.3
  481.1 155.1 %all-to-all-done.2 = bf16[32,40,2880]{2,1,0:T(8,128)(2,1)} async-done(((bf16[32,40,2880]{2,1,0:T(8,128)(2,1)}), bf16[32,40,2880]{2,1,0:T(8,128)(2,1)}, u32[]{:S(2)}, u32[]{:S(2)}) %all-to-all-start.2) | async-done | bytes 7372832 | tf_op jit(solution)/shard_map/all_to_all | solution.py:165
  636.2 6.4 fusion.25
  643.8 6.9 %fusion.11 = bf16[128,2880]{0,1:T(8,128)(2,1)} fusion(f32[128,2880]{0,1:T(8,128)S(1)} %fusion.30, bf16[1280,2880]{1,0:T(8,128)(2,1)} %bitcast.25, bf16[128,2880]{0,1:T(8,128)(2,1)S(1)} %copy-done.5, f32[128]{0:T(128)S(1)} %get-tuple-element.25, f32[128]{0:T(128)S(1)} %get-tuple-element.26, f32[128]{0:T(128)S(1)} %get-tuple-element.27, ...), kind=kOutput, calls=%fused_computation.23 | convolution fusion | flops 948305920 | bytes 10328064 | tf_op jit(solution)/shard_map/dot_general | solution.py:184
  650.8 1.3 fusion.18
  (42 shorter events, 5.2 us)
Async XLA Ops:
  0.6 3.1 copy-start
  5.4 6.0 copy-start.6
  208.9 10.2 %copy-start.8 = (s32[1,720,90]{1,0,2:T(1,128)S(1)}, s32[1,720,90]{1,0,2:T(1,128)}, u32[]{:S(2)}) copy-start(s32[1,720,90]{1,0,2:T(1,128)} %param.16) | copy-start | bytes 777604
  208.9 10.7 %copy-start.7 = (s32[1,90,1440]{2,0,1:T(1,128)S(1)}, s32[1,90,1440]{2,0,1:T(1,128)}, u32[]{:S(2)}) copy-start(s32[1,90,1440]{2,0,1:T(1,128)} %param.14) | copy-start | bytes 1555204
  219.1 31.3 %collective-permute-start = (bf16[1280,2880]{0,1:T(8,128)(2,1)}, bf16[1280,2880]{0,1:T(8,128)(2,1)}, u32[]{:S(2)}, u32[]{:S(2)}) collective-permute-start(bf16[1280,2880]{0,1:T(8,128)(2,1)} %copy.43), channel_id=1, source_target_pairs={{0,1},{1,0},{2,3},{3,2},{4,5},{5,4},{6,7},{7,6},{8,9},{9,8},{10,11... | collective-permute-start | bytes 22118408 | tf_op jit(solution)/shard_map/ppermute | solution.py:157
  227.6 2.3 copy-start.1
  235.0 37.1 %copy-start.4 = (bf16[2880,720]{1,0:T(8,128)(2,1)}, bf16[2880,720]{1,0:T(8,128)(2,1)S(1)}, u32[]{:S(2)}) copy-start(bf16[2880,720]{1,0:T(8,128)(2,1)S(1)} %shard_map.105) | copy-start | bytes 12441604
  235.0 5.1 copy-start.2
  250.3 21.8 %copy-start.3 = (bf16[2880,1440]{1,0:T(8,128)(2,1)}, bf16[2880,1440]{1,0:T(8,128)(2,1)S(1)}, u32[]{:S(2)}) copy-start(bf16[2880,1440]{1,0:T(8,128)(2,1)S(1)} %shard_map.104) | copy-start | bytes 24883204
  272.2 2.9 copy-start.10
  294.0 171.1 %all-to-all-start.1 = ((bf16[32,40,2880]{2,1,0:T(8,128)(2,1)}), bf16[32,40,2880]{2,1,0:T(8,128)(2,1)}, u32[]{:S(2)}, u32[]{:S(2)}) async-start(bf16[32,40,2880]{2,1,0:T(8,128)(2,1)} %bitcast.72), calls=%async_computation.1 | async-start | bytes 15073280 | tf_op jit(solution)/shard_map/all_to_all | solution.py:162
  465.1 171.1 %all-to-all-start.2 = ((bf16[32,40,2880]{2,1,0:T(8,128)(2,1)}), bf16[32,40,2880]{2,1,0:T(8,128)(2,1)}, u32[]{:S(2)}, u32[]{:S(2)}) async-start(bf16[32,40,2880]{2,1,0:T(8,128)(2,1)} %bitcast.71), calls=%async_computation.2 | async-start | bytes 15073280 | tf_op jit(solution)/shard_map/all_to_all | solution.py:165
  636.2 6.4 copy-start.9
  636.2 6.5 copy-start.5
